TPU v7x, 256 devices: a whole 4x4x8 slice. The times are simulated.
256 devices in a mesh: row: 4 (over x), vocab: 64 (over y, z, core).
Axes of the slice: x: 4, y: 4, z: 8, core: 2. Of those that a mesh axis runs over, the one named last changes fastest.
Arguments:
- teacher_hidden: bfloat16 [512, 4608], P('vocab', 'row'), may hold values from -35 to 35
- student_hidden: bfloat16 [512, 3584], P('vocab', 'row'), may hold values from -35 to 35
- teacher_weight: bfloat16 [4608, 128000], P('row', 'vocab'), may hold values from -0.1875 to 0.1875
- student_weight: bfloat16 [3584, 128000], P('row', 'vocab'), may hold values from -0.1875 to 0.1875
- sampled_ids: int32 [512], P('row'), may hold values from 0 to 127999
Outputs:
- reverse_kl: float32 [512], P('row')
- chosen_logprob: float32 [2, 512], P(None, 'row')
- logit_grad: bfloat16 [512, 128000], P('row', 'vocab')
- weight_grad: bfloat16 [3584, 128000], P('row', 'vocab')
- hidden_grad: bfloat16 [512, 3584], P('vocab', 'row')
All inputs are finite; a program needn't handle non-finite values.
Results may differ from a plain program's by a relative error of at most 0.01.
Values may be sent and summed in bfloat16 or wider, within the bound.
A program may use at most 128 MiB of HBM per device.

v0:
```python
import jax
import jax.numpy as jnp
from jax import lax
from jax.sharding import PartitionSpec as P


def softcap(values):
    return 30.0 * jnp.tanh(values / 30.0)


def project(columns, weight):
    return jnp.dot(columns, weight, preferred_element_type=jnp.float32)


def project_back(gradient, weight):
    return lax.dot_general(
        gradient, weight, (((1,), (1,)), ((), ())), preferred_element_type=jnp.float32
    )


def body(teacher_hidden, student_hidden, teacher_weight, student_weight, sampled_ids):
    teacher_columns, student_columns = (
        lax.all_gather(teacher_hidden, "vocab", axis=0, tiled=True),
        lax.all_gather(student_hidden, "vocab", axis=0, tiled=True),
    )
    rows_here = sampled_ids.shape[0]
    vocab_width = teacher_weight.shape[1]
    teacher_raw = lax.psum_scatter(
        project(teacher_columns, teacher_weight), "row", scatter_dimension=0, tiled=True
    )
    teacher_logits = softcap(teacher_raw)
    offset = lax.axis_index("vocab") * vocab_width
    positions = lax.broadcasted_iota(jnp.int32, (rows_here, vocab_width), 1)
    matches = positions == (sampled_ids - offset)[:, None]
    teacher_part = jnp.sum(jnp.exp(teacher_logits), axis=1)
    teacher_hit = jnp.sum(jnp.where(matches, teacher_logits, 0.0), axis=1)
    student_raw = lax.psum_scatter(
        project(student_columns, student_weight), "row", scatter_dimension=0, tiled=True
    )
    student_logits = softcap(student_raw)
    student_exp = jnp.exp(student_logits)
    student_part = jnp.sum(student_exp, axis=1)
    cross_part = jnp.sum(student_exp * (student_logits - teacher_logits), axis=1)
    student_hit = jnp.sum(jnp.where(matches, student_logits, 0.0), axis=1)
    teacher_total, teacher_pick, student_total, cross, student_pick = lax.psum(
        (teacher_part, teacher_hit, student_part, cross_part, student_hit), "vocab"
    )
    student_log = jnp.log(student_total)
    teacher_log = jnp.log(teacher_total)
    divergence = cross / student_total - student_log + teacher_log
    chosen = jnp.stack([student_pick - student_log, teacher_pick - teacher_log])
    probs = student_exp / student_total[:, None]
    shifted = (
        student_logits
        - teacher_logits
        - student_log[:, None]
        + teacher_log[:, None]
        - divergence[:, None]
    )
    logit_grad = (probs * shifted * (1.0 - (student_logits / 30.0) ** 2)).astype(jnp.bfloat16)
    grad_rows = lax.all_gather(logit_grad, "row", axis=0, tiled=True)
    weight_grad = lax.dot_general(
        student_columns, grad_rows, (((0,), (0,)), ((), ())), preferred_element_type=jnp.float32
    ).astype(jnp.bfloat16)
    hidden_grad = lax.psum_scatter(
        project_back(grad_rows, student_weight), "vocab", scatter_dimension=0, tiled=True
    )
    return (divergence, chosen, logit_grad, weight_grad, hidden_grad.astype(jnp.bfloat16))


def solution(mesh):
    placed = (P("vocab", "row"), P("vocab", "row"), P("row", "vocab"), P("row", "vocab"), P("row"))
    return jax.shard_map(
        body,
        mesh=mesh,
        in_specs=placed,
        out_specs=(
            P("row"),
            P(None, "row"),
            P("row", "vocab"),
            P("row", "vocab"),
            P("vocab", "row"),
        ),
        check_vma=False,
    )
```

profile of v0, /device:TPU:1, one launch (start us, length us, event | category | flops | bytes accessed | tf_op | source)
XLA Modules:
  0.0 615.6 jit_solution(16984500588053771233)
XLA Ops:
  8.0 0.0 all-gather.3.cloned.1.call-start
  8.0 0.7 all-gather.3.cloned.1.call-update
  8.7 0.0 reduce-scatter.3.cloned.1.call-start
  8.8 55.3 %all_gather.9 = bf16[512,896]{1,0:T(8,128)(2,1)S(1)} all-gather(bf16[8,896]{1,0:T(8,128)(2,1)} %param.6), channel_id=1, replica_groups=mesh['row'=4,'vocab'=64] {'vocab'}, dimensions={0}, use_global_device_ids=true | all-gather | bytes 931840 | tf_op jit(solution)/shard_map/all_gather | solution.py:24
  64.1 6.2 %fusion.4 = f32[512,2000]{0,1:T(8,128)} fusion(bf16[512,896]{1,0:T(8,128)(2,1)S(1)} %all_gather.9, bf16[896,2000]{0,1:T(8,128)(2,1)} %param.8), kind=kOutput, calls=%fused_computation.20 | convolution fusion | flops 1835008000 | bytes 8597504 | tf_op jit(solution)/shard_map/dot_general | solution.py:12
  70.3 0.0 reduce-scatter.3.cloned.1.call-update
  70.4 0.0 reduce-scatter.5.cloned.1.call-start
  70.4 22.2 %all-gather.3.cloned.1.call-done = bf16[512,1152]{1,0:T(8,128)(2,1)} async-done(((bf16[8,1152]{1,0:T(8,128)(2,1)}), bf16[512,1152]{1,0:T(8,128)(2,1)}) %all-gather.3.cloned.1.call-update) | async-done | bytes 1179664 | tf_op jit(solution)/shard_map/all_gather | solution.py:23
  92.6 7.5 %fusion.5 = f32[512,2000]{0,1:T(8,128)} fusion(bf16[512,1152]{1,0:T(8,128)(2,1)} %all-gather.3.cloned.1.call-done, bf16[1152,2000]{0,1:T(8,128)(2,1)} %param.7), kind=kOutput, calls=%fused_computation.21 | convolution fusion | flops 2359296000 | bytes 9883648 | tf_op jit(solution)/shard_map/dot_general | solution.py:12
  100.1 0.0 copy-start.1
  100.1 0.0 reduce-scatter.5.cloned.1.call-update
  100.2 0.0 copy-start.2
  100.2 0.0 all-gather.5.cloned.1.call-start
  100.2 0.6 copy-done.1
  100.8 15.2 %reduce-scatter.3.cloned.1.call-done = f32[128,2000]{0,1:T(8,128)} async-done(((f32[512,2000]{0,1:T(8,128)}), f32[128,2000]{0,1:T(8,128)}) %reduce-scatter.3.cloned.1.call-update) | async-done | bytes 1024016 | tf_op jit(solution)/shard_map/reduce_scatter | solution.py:37
  116.0 50.9 %reduce-scatter.5.cloned.1.call-done = f32[128,2000]{0,1:T(8,128)} async-done(((f32[512,2000]{0,1:T(8,128)}), f32[128,2000]{0,1:T(8,128)}) %reduce-scatter.5.cloned.1.call-update) | async-done | bytes 1024016 | tf_op jit(solution)/shard_map/reduce_scatter | solution.py:28
  166.8 2.2 select_reduce_fusion.1
  169.1 124.7 %all-reduce.2 = (f32[128]{0:T(128)S(1)}, f32[128]{0:T(128)S(1)}, f32[128]{0:T(128)S(1)}) all-reduce(f32[128]{0:T(128)S(1)} %get-tuple-element.7, f32[128]{0:T(128)S(1)} %get-tuple-element.6, f32[128]{0:T(128)S(1)} %get-tuple-element.9), channel_id=1, replica_groups=mesh['row'=4,'vocab'=64] {'vocab'}, use_global_device_ids=true, to_apply=%region_3.4 | all-reduce | flops 384 | bytes 3072 | tf_op jit(solution)/shard_map/psum | solution.py:45
  293.7 0.0 copy-start
  293.7 2.9 multiply_convert_fusion
  296.7 0.0 all-gather.5.cloned.1.call-update
  296.7 0.0 copy-done.2
  296.7 0.6 dynamic-slice
  297.9 30.4 %all-gather.5.cloned.1.call-done = bf16[512,2000]{0,1:T(8,128)(2,1)} async-done(((bf16[128,2000]{0,1:T(8,128)(2,1)}), bf16[512,2000]{0,1:T(8,128)(2,1)}) %all-gather.5.cloned.1.call-update) | async-done | bytes 2048016 | tf_op jit(solution)/shard_map/all_gather | solution.py:61
  328.3 5.0 fusion.6
  333.3 0.0 copy-done
  333.3 267.1 %all-reduce.4 = (f32[128]{0:T(128)S(1)}, f32[128]{0:T(128)S(1)}, bf16[512,896]{1,0:T(8,128)(2,1)}) all-reduce(f32[128]{0:T(128)S(1)} %get-tuple-element.8, f32[128]{0:T(128)S(1)} %get-tuple-element.5, f32[512,896]{1,0:T(8,128)S(1)} %fusion.6), channel_id=1, replica_groups=mesh['row'=4,'vocab'=64] {'vocab'}, use_global_device_ids=true, to_apply=%region_11.12 | all-reduce | flops 459008 | bytes 2754560 | tf_op jit(solution)/shard_map/psum | solution.py:45
  600.4 0.6 pad_maximum_fusion
  601.0 1.3 dynamic-slice_convert_fusion
  602.3 5.7 fusion
  (3 shorter events, 0.0 us)
Async XLA Ops:
  8.0 84.6 %all-gather.3.cloned.1.call-start = ((), (), s32[]{:S(2)}) async-start(), calls=%async_computation.3 | async-start | bytes 1198080 | tf_op jit(solution)/shard_map/all_gather | solution.py:23
  8.7 107.2 %reduce-scatter.3.cloned.1.call-start = ((), (), s32[]{:S(2)}) async-start(), calls=%async_computation.2 | async-start | bytes 5120000 | tf_op jit(solution)/shard_map/reduce_scatter | solution.py:37
  70.4 96.5 %reduce-scatter.5.cloned.1.call-start = ((), (), s32[]{:S(2)}) async-start(), calls=%async_computation.4 | async-start | bytes 5120000 | tf_op jit(solution)/shard_map/reduce_scatter | solution.py:28
  100.1 0.7 copy-start.1
  100.2 196.5 %copy-start.2 = (u32[256]{0:T(256)S(1)}, u32[256]{0:T(256)}, u32[]{:S(2)}) copy-start(u32[256]{0:T(256)} %constant.23) | copy-start | bytes 3076
  100.2 228.1 %all-gather.5.cloned.1.call-start = ((), (), s32[]{:S(2)}) async-start(), calls=%async_computation.5 | async-start | bytes 2560000 | tf_op jit(solution)/shard_map/all_gather | solution.py:61
  293.7 39.5 %copy-start = (f32[128]{0:T(128)}, f32[128]{0:T(128)S(1)}, u32[]{:S(2)}) copy-start(f32[128]{0:T(128)S(1)} %get-tuple-element.17) | copy-start | bytes 1540
Sparse Core Ops, SparseCore 0:
  11.9 80.6 all-gather.2
Sparse Core Ops, SparseCore 1:
  70.4 45.5 reduce-scatter.2
  118.6 48.2 reduce-scatter.4
  296.8 31.5 all-gather.4
where the time goes:
time: 620 us; the launch traced here: 616 us
  blocking collectives  447 us (72%)
  waiting for transfers between devices  119 us (19%)
  matrix products  24.4 us (4%)
  between operations  16.4 us (3%)
    psum x2, blocking collectives, body(): lax.psum((teacher_part, teacher_hit, student_part, cross_part, student_hi...  392 us
    all_gather x1, blocking collectives, body(): lax.all_gather(student_hidden, 'vocab', axis=0, tiled=True)  55.3 us
    reduce_scatter x1, waiting for transfers between devices, body(): lax.psum_scatter(project(teacher_columns, teacher_weight), 'row', scatter...  50.9 us
    all_gather x1, waiting for transfers between devices, body(): grad_rows = lax.all_gather(logit_grad, 'row', axis=0, tiled=True)  30.4 us
    all_gather x1, waiting for transfers between devices, body(): lax.all_gather(teacher_hidden, 'vocab', axis=0, tiled=True)  22.2 us
    reduce_scatter x1, waiting for transfers between devices, body(): lax.psum_scatter(project(student_columns, student_weight), 'row', scatter...  15.2 us
    dot_general x2, matrix products, project(): return jnp.dot(columns, weight, preferred_element_type=jnp.float32)  13.8 us
  transfers between devices with their start and end apart: 4, of which 4 were waited for; matrix products, arithmetic and copies ran while one was open for 2% of the time, Pallas kernels for 0%

commit v1 on v0

v1 whole, which is shorter than its diff:
```python
import jax
import jax.numpy as jnp
from jax import lax
from jax.experimental import pallas as pl
from jax.experimental.pallas import tpu as pltpu
from jax.sharding import PartitionSpec as P

MESH = pl.DeviceIdType.MESH
F32, BF16, I16 = jnp.float32, jnp.bfloat16, jnp.int16
NX, NY, NZ, NC = 4, 4, 8, 2
HALVES = 2
ROWS = 64
COLS = 2000
WIDE = 2048
TAIL = WIDE - 128
GROUP = 16
SCALE = 32000.0
BLOCKS = ((0, 512), (512, 1024), (1024, 1536), (1536, COLS))


def softcap(values):
    return 30.0 * jnp.tanh(values * (1.0 / 30.0))


def encode(values, ref, at):
    most = jnp.max(jnp.abs(values), axis=1, keepdims=True)
    power = jnp.ceil(jnp.log2(jnp.maximum(most, 1e-30)))
    whole = jnp.round(values * (jnp.exp2(-power) * SCALE))
    lane = lax.broadcasted_iota(jnp.int32, (values.shape[0], 128), 1)
    last = jnp.where(lane >= COLS - TAIL, power, whole[:, TAIL:])
    ref[at, 0:TAIL] = whole[:, :TAIL].astype(I16)
    ref[at, TAIL:WIDE] = last.astype(I16)


def decode(ref, at):
    values = ref[at, :].astype(F32)
    lane = lax.broadcasted_iota(jnp.int32, (values.shape[0], 128), 1)
    power = jnp.max(jnp.where(lane >= COLS - TAIL, values[:, TAIL:], -1000.0), axis=1, keepdims=True)
    return values * (jnp.exp2(power) * (1.0 / SCALE))


def kernel(
    th, sh, ids, wt_hbm, ws_hbm,
    kl_out, chosen_out, grad_out, wg_out, hg_out,
    wt, ws, ht, hs, lt, ls, part, one_s, one_r, two_s, two_r, logits, stat, ids_at, sr1, sr2, res, res_at, back,
    grads, wg_acc, wg_stage, hp, hc, ysum, yr, zs, zr,
    w_sem, zsnd, zrcv, ysnd, yrcv, csnd, crcv,
    one_ss, one_rs, two_ss, two_rs, s1_ss, s1_rs, s2_ss, s2_rs, g_ss, g_rs, f_ss, f_rs,
    hc_ss, hc_rs, hy_ss, hy_rs, hz_ss, hz_rs, out_sem,
):
    x = lax.axis_index("row")
    v = lax.axis_index("vocab")
    y, z, c = v // 16, (v // 2) % 8, v % 2
    right, left, across = (x + 1) % 4, (x + 3) % 4, (x + 2) % 4

    def at_x(to):
        return (to, v)

    def at_v(ty, tz, tc):
        return (x, ty * 16 + tz * 2 + tc)

    def remote(src, dst, ss, rs, device):
        return pltpu.make_async_remote_copy(
            src_ref=src, dst_ref=dst, send_sem=ss, recv_sem=rs, device_id=device, device_id_type=MESH
        )

    def landed(ref, sem):
        remote(ref, ref, sem, sem, at_x(right)).wait_recv()

    def left_here(ref, sem):
        remote(ref, ref, sem, sem, at_x(right)).wait_send()

    load_s = pltpu.make_async_copy(ws_hbm, ws, w_sem.at[0])
    load_t = pltpu.make_async_copy(wt_hbm, wt, w_sem.at[1])
    load_s.start()
    load_t.start()

    barrier = pltpu.get_barrier_semaphore()
    for to in (right, left):
        pl.semaphore_signal(barrier, inc=1, device_id=at_x(to), device_id_type=MESH)
    for step in range(1, 8):
        pl.semaphore_signal(
            barrier, inc=1, device_id=at_v((y + step // 2) % 4, z, (c + step) % 2), device_id_type=MESH
        )
        pl.semaphore_signal(barrier, inc=1, device_id=at_v(y, (z + step) % 8, c), device_id_type=MESH)

    hs[y, z, c] = sh[...]
    ht[y, z, c] = th[...]
    part[:, :, TAIL:WIDE] = jnp.zeros((3, ROWS, 128), F32)
    stat[...] = jnp.zeros((128, 128), F32)
    res[...] = jnp.zeros((128, 128), F32)
    ids_at[...] = jnp.transpose(jnp.broadcast_to(ids[...].astype(F32), (128, 128)))

    pl.semaphore_wait(barrier, 16)

    both = ((0, hs), (1, ht))
    for m, ref in both:
        for step in range(1, 8):
            to = (z + step) % 8
            remote(
                ref.at[y, z, c], ref.at[y, z, c], zsnd.at[m, step], zrcv.at[m, z], at_v(y, to, c)
            ).start()

    def z_arrive(m, ref, half):
        for k in range(4):
            zz = 4 * half + k

            @pl.when(zz != z)
            def _():
                landed(ref.at[y, zz, c], zrcv.at[m, zz])

    def y_send(m, ref, half):
        src = ref.at[y, pl.ds(4 * half, 4), c]
        for step in (1, 3, 2):
            remote(
                src, src, ysnd.at[m, half, step], yrcv.at[m, half, y], at_v((y + step) % 4, z, c)
            ).start()

    def y_arrive(m, ref, half):
        for step in (1, 3, 2):
            yy = (y + step) % 4
            landed(ref.at[yy, pl.ds(4 * half, 4), c], yrcv.at[m, half, yy])

    def c_send(m, ref, half):
        src = ref.at[:, pl.ds(4 * half, 4), c]
        remote(src, src, csnd.at[m, half], crcv.at[m, half], at_v(y, z, 1 - c)).start()

    def c_arrive(m, ref, half):
        landed(ref.at[:, pl.ds(4 * half, 4), 1 - c], crcv.at[m, half])

    def layout(m, ref, rows, half):
        wide = rows.shape[-1]
        for k in range(4):
            block = ref[k, 4 * half : 4 * half + 4].astype(F32)
            rows[half, k] = block.reshape(ROWS, wide).astype(BF16)

    def product(m, half, chunk, slot):
        rows, weight = (ls, ws) if m == 0 else (lt, wt)
        lhs = rows[half, chunk]
        for lo, hi in BLOCKS:
            part[slot, :, lo:hi] = jnp.dot(lhs, weight[:, lo:hi], preferred_element_type=F32)

    def hop_one(m, half):
        u = 2 * half + m
        product(m, half, across, 0)

        @pl.loop(0, ROWS // GROUP)
        def _(g):
            at = pl.ds(pl.multiple_of(g * GROUP, GROUP), GROUP)
            encode(part[0, at, :], one_s.at[u], at)

        remote(
            one_s.at[u, pl.ds(0, 32)], one_r.at[u, 0], one_ss.at[u, 0], one_rs.at[u, 0], at_x(right)
        ).start()
        remote(
            one_s.at[u, pl.ds(32, 32)], one_r.at[u, 1], one_ss.at[u, 1], one_rs.at[u, 1], at_x(left)
        ).start()

    def hop_two(m, half):
        u = 2 * half + m
        for side, chunk, to in ((0, right, right), (1, left, left)):
            product(m, half, chunk, 1 + side)
        for side, to in ((0, right), (1, left)):
            landed(one_r.at[u, side], one_rs.at[u, side])

            @pl.loop(0, 2)
            def _(g):
                inner = pl.ds(pl.multiple_of(g * GROUP, GROUP), GROUP)
                at = pl.ds(pl.multiple_of(side * 32 + g * GROUP, GROUP), GROUP)
                plain = pl.ds(pl.multiple_of((1 - side) * 32 + g * GROUP, GROUP), GROUP)
                encode(part[1 + side, at, :] + decode(one_r.at[u, side], inner), two_s.at[u, side], at)
                encode(part[1 + side, plain, :], two_s.at[u, side], plain)

            remote(
                two_s.at[u, side], two_r.at[u, side], two_ss.at[u, side], two_rs.at[u, side], at_x(to)
            ).start()

    def finish(m, half):
        u = 2 * half + m
        product(m, half, x, 0)
        for side in (0, 1):
            landed(two_r.at[u, side], two_rs.at[u, side])
        column = lax.broadcasted_iota(jnp.int32, (GROUP, WIDE), 1)
        lane = lax.broadcasted_iota(jnp.int32, (GROUP, 128), 1)

        @pl.loop(0, ROWS // GROUP)
        def _(g):
            at = pl.ds(pl.multiple_of(g * GROUP, GROUP), GROUP)
            raw = part[0, at, :] + decode(two_r.at[u, 0], at) + decode(two_r.at[u, 1], at)
            capped = softcap(raw)
            logits[half, m, at, :] = capped
            if m == 1:
                here = pl.ds(pl.multiple_of(half * ROWS + g * GROUP, GROUP), GROUP)
                student = logits[half, 0, at, :]
                valid = column < COLS
                t_exp = jnp.where(valid, jnp.exp(capped), 0.0)
                s_exp = jnp.where(valid, jnp.exp(student), 0.0)
                wanted = ids_at[here, 0:1].astype(jnp.int32) - v * COLS
                hit = jnp.logical_and(column == wanted, valid)
                sums = (
                    t_exp,
                    jnp.where(hit, capped, 0.0),
                    s_exp,
                    s_exp * (student - capped),
                    jnp.where(hit, student, 0.0),
                )
                tile = jnp.zeros((GROUP, 128), F32)
                for j, term in enumerate(sums):
                    tile = jnp.where(lane == j, jnp.sum(term, axis=1, keepdims=True), tile)
                stat[here, :] = tile

    group = y * 2 + c

    def stats_one(half):
        sr1[half, group] = jnp.transpose(stat[...])[0:8, :]
        for step in range(1, 8):
            remote(
                sr1.at[half, group], sr1.at[half, group], s1_ss.at[half, step], s1_rs.at[half, group],
                at_v((y + step // 2) % 4, z, (c + step) % 2),
            ).start()

    def stats_two(half):
        for step in range(1, 8):
            who = ((y + step // 2) % 4) * 2 + (c + step) % 2
            landed(sr1.at[half, who], s1_rs.at[half, who])
        total = sr1[half, 0]
        for k in range(1, 8):
            total = total + sr1[half, k]
        sr2[half, z] = total
        for step in range(1, 8):
            remote(
                sr2.at[half, z], sr2.at[half, z], s2_ss.at[half, step], s2_rs.at[half, z],
                at_v(y, (z + step) % 8, c),
            ).start()

    def gradient(half):
        for step in range(1, 8):
            who = (z + step) % 8
            landed(sr2.at[half, who], s2_rs.at[half, who])
        total = sr2[half, 0]
        for k in range(1, 8):
            total = total + sr2[half, k]
        t_total, t_pick, s_total, cross, s_pick = (total[j : j + 1, :] for j in range(5))
        s_log, t_log = jnp.log(s_total), jnp.log(t_total)
        divergence = cross / s_total - s_log + t_log
        res[0:1, :] = 1.0 / s_total
        res[1:2, :] = t_log - s_log - divergence
        back[half, 0:1, :] = divergence
        back[half, 1:2, :] = s_pick - s_log
        back[half, 2:3, :] = t_pick - t_log
        res_at[...] = jnp.transpose(res[...])

        @pl.loop(0, ROWS // GROUP)
        def _(g):
            at = pl.ds(pl.multiple_of(g * GROUP, GROUP), GROUP)
            here = pl.ds(pl.multiple_of(half * ROWS + g * GROUP, GROUP), GROUP)
            student, teacher = logits[half, 0, at, :], logits[half, 1, at, :]
            inverse, shift = res_at[here, 0:1], res_at[here, 1:2]
            ratio = student * (1.0 / 30.0)
            value = (
                jnp.exp(student) * inverse * (student - teacher + shift) * (1.0 - ratio * ratio)
            ).astype(BF16)
            grads[half, x, at, :] = value
            grad_out[here, :] = value[:, :COLS]

        mine = grads.at[half, x]
        remote(mine, mine, g_ss.at[half, 0], g_rs.at[half, 0], at_x(right)).start()
        remote(mine, mine, g_ss.at[half, 1], g_rs.at[half, 1], at_x(left)).start()

    def forward(half):
        landed(grads.at[half, left], g_rs.at[half, 0])
        src = grads.at[half, left, pl.ds(0, 32)]
        remote(src, src, f_ss.at[half, 0], f_rs.at[half, 0], at_x(right)).start()
        landed(grads.at[half, right], g_rs.at[half, 1])
        src = grads.at[half, right, pl.ds(32, 32)]
        remote(src, src, f_ss.at[half, 1], f_rs.at[half, 1], at_x(left)).start()

    def gathered(half):
        landed(grads.at[half, across, pl.ds(0, 32)], f_rs.at[half, 0])
        landed(grads.at[half, across, pl.ds(32, 32)], f_rs.at[half, 1])

    def all_rows(half):
        return grads[half, :, :, 0:COLS].reshape(NX * ROWS, COLS)

    def hidden_product(half):
        rows = all_rows(half)
        for lo, hi in ((0, 256), (256, 512), (512, 768), (768, 896)):
            block = lax.dot_general(
                rows, ws[lo:hi, :], (((1,), (1,)), ((), ())), preferred_element_type=F32
            )
            hp[half, :, :, :, :, lo:hi] = block.reshape(4, 4, 2, 8, hi - lo)
        remote(
            hp.at[half, :, :, 1 - c], hc.at[half], hc_ss.at[half], hc_rs.at[half], at_v(y, z, 1 - c)
        ).start()

    def weight_product(half):
        rows = all_rows(half)

        @pl.loop(0, 7)
        def _(i):
            at = pl.ds(pl.multiple_of(i * 128, 128), 128)
            lhs = ls[half, :, :, at].reshape(NX * ROWS, 128)
            block = lax.dot_general(lhs, rows, (((0,), (0,)), ((), ())), preferred_element_type=F32)
            if half == 0:
                wg_acc[at, :] = block
            else:
                wg_stage[at, :] = (wg_acc[at, :] + block).astype(BF16)

    def hidden_y(half):
        landed(hc.at[half], hc_rs.at[half])
        for k in range(4):
            total = hp[half, k, :, c] + hc[half, k]
            ysum[half, k] = total.reshape(32, 896).astype(BF16)
        for step in (1, 3, 2):
            to = (y + step) % 4
            remote(
                ysum.at[half, to], yr.at[half, step], hy_ss.at[half, step], hy_rs.at[half, step],
                at_v(to, z, c),
            ).start()

    def hidden_z(half):
        total = ysum[half, y].astype(F32)
        for step in (1, 2, 3):
            landed(yr.at[half, step], hy_rs.at[half, step])
            total = total + yr[half, step].astype(F32)
        zs[half] = total.reshape(4, 8, 896)
        for k in range(4):
            zz = 4 * half + k

            @pl.when(zz != z)
            def _():
                remote(
                    zs.at[half, k], zr.at[z], hz_ss.at[half, k], hz_rs.at[z], at_v(y, zz, c)
                ).start()

    def hidden_end(half):
        @pl.when(z // 4 == half)
        def _():
            zr[z] = zs[half, z % 4]
            for step in range(1, 8):
                who = (z + step) % 8
                landed(zr.at[who], hz_rs.at[who])
            total = zr[0]
            for k in range(1, 8):
                total = total + zr[k]
            hg_out[...] = total.astype(BF16)

    for m, ref in both:
        for half in range(HALVES):
            z_arrive(m, ref, half)
            y_send(m, ref, half)
    for half in range(HALVES):
        y_arrive(0, hs, half)
        c_send(0, hs, half)
    c_arrive(0, hs, 0)
    layout(0, hs, ls, 0)
    load_s.wait()
    hop_one(0, 0)
    c_arrive(0, hs, 1)
    layout(0, hs, ls, 1)
    for half in range(HALVES):
        y_arrive(1, ht, half)
        c_send(1, ht, half)
    load_t.wait()
    c_arrive(1, ht, 0)
    layout(1, ht, lt, 0)
    hop_one(1, 0)
    c_arrive(1, ht, 1)
    layout(1, ht, lt, 1)
    hop_two(0, 0)
    hop_one(0, 1)
    hop_two(1, 0)
    hop_one(1, 1)
    finish(0, 0)
    hop_two(0, 1)
    finish(1, 0)
    stats_one(0)
    hop_two(1, 1)
    stats_two(0)
    finish(0, 1)
    gradient(0)
    finish(1, 1)
    stats_one(1)
    forward(0)
    stats_two(1)
    gathered(0)
    hidden_product(0)
    gradient(1)
    hidden_y(0)
    weight_product(0)
    hidden_z(0)
    forward(1)
    hidden_end(0)
    gathered(1)
    hidden_product(1)
    weight_product(1)
    store = pltpu.make_async_copy(wg_stage, wg_out, out_sem)
    store.start()
    hidden_y(1)
    hidden_z(1)
    lane = lax.broadcasted_iota(jnp.int32, (1, 128), 1)
    kl_out[...] = jnp.where(lane < ROWS, back[0, 0:1, :], back[1, 0:1, :])
    chosen_out[...] = jnp.where(lane < ROWS, back[0, 1:3, :], back[1, 1:3, :])
    hidden_end(1)
    store.wait()

    for m, ref in both:
        for step in range(1, 8):
            left_here(ref.at[y, z, c], zsnd.at[m, step])
        for half in range(HALVES):
            for step in (1, 2, 3):
                left_here(ref.at[y, pl.ds(4 * half, 4), c], ysnd.at[m, half, step])
            left_here(ref.at[:, pl.ds(4 * half, 4), c], csnd.at[m, half])
    for u in range(4):
        for side in (0, 1):
            left_here(one_s.at[u, pl.ds(0, 32)], one_ss.at[u, side])
            left_here(two_s.at[u, side], two_ss.at[u, side])
    for half in range(HALVES):
        for step in range(1, 8):
            left_here(sr1.at[half, group], s1_ss.at[half, step])
            left_here(sr2.at[half, z], s2_ss.at[half, step])
        for side in (0, 1):
            left_here(grads.at[half, x], g_ss.at[half, side])
            left_here(grads.at[half, x, pl.ds(0, 32)], f_ss.at[half, side])
        left_here(hc.at[half], hc_ss.at[half])
        for step in (1, 2, 3):
            left_here(ysum.at[half, 0], hy_ss.at[half, step])
        for k in range(4):

            @pl.when(4 * half + k != z)
            def _():
                left_here(zs.at[half, k], hz_ss.at[half, k])


def body(teacher_hidden, student_hidden, teacher_weight, student_weight, sampled_ids):
    dma, vmem = pltpu.SemaphoreType.DMA, pltpu.VMEM
    on_chip = pl.BlockSpec(memory_space=pltpu.VMEM)
    any_space = pl.BlockSpec(memory_space=pl.ANY)
    kt, ks = teacher_weight.shape[0], student_weight.shape[0]
    outs = (
        jax.ShapeDtypeStruct((1, 128), F32),
        jax.ShapeDtypeStruct((2, 128), F32),
        jax.ShapeDtypeStruct((128, COLS), BF16),
        jax.ShapeDtypeStruct((ks, COLS), BF16),
        jax.ShapeDtypeStruct((8, ks), BF16),
    )
    kl, chosen, grad, weight_grad, hidden_grad = pl.pallas_call(
        kernel,
        out_shape=outs,
        in_specs=[on_chip, on_chip, on_chip, any_space, any_space],
        out_specs=(on_chip, on_chip, on_chip, any_space, on_chip),
        scratch_shapes=[
            vmem((kt, COLS), BF16), vmem((ks, COLS), BF16),
            vmem((4, 8, 2, 8, kt), BF16), vmem((4, 8, 2, 8, ks), BF16),
            vmem((2, 4, ROWS, kt), BF16), vmem((2, 4, ROWS, ks), BF16),
            vmem((3, ROWS, WIDE), F32),
            vmem((4, ROWS, WIDE), I16), vmem((4, 2, 32, WIDE), I16),
            vmem((4, 2, ROWS, WIDE), I16), vmem((4, 2, ROWS, WIDE), I16),
            vmem((2, 2, ROWS, WIDE), F32),
            vmem((128, 128), F32), vmem((128, 128), F32),
            vmem((2, 8, 8, 128), F32), vmem((2, 8, 8, 128), F32),
            vmem((128, 128), F32), vmem((128, 128), F32), vmem((2, 8, 128), F32),
            vmem((2, 4, ROWS, WIDE), BF16),
            vmem((ks, COLS), F32), vmem((ks, COLS), BF16),
            vmem((2, 4, 4, 2, 8, ks), F32), vmem((2, 4, 4, 8, ks), F32),
            vmem((2, 4, 32, ks), BF16), vmem((2, 4, 32, ks), BF16),
            vmem((2, 4, 8, ks), F32), vmem((8, 8, ks), F32),
            dma((2,)), dma((2, 8)), dma((2, 8)), dma((2, 2, 4)), dma((2, 2, 4)), dma((2, 2)), dma((2, 2)),
            dma((4, 2)), dma((4, 2)), dma((4, 2)), dma((4, 2)),
            dma((2, 8)), dma((2, 8)), dma((2, 8)), dma((2, 8)),
            dma((2, 2)), dma((2, 2)), dma((2, 2)), dma((2, 2)),
            dma((2,)), dma((2,)), dma((2, 4)), dma((2, 4)), dma((2, 4)), dma((8,)), dma(()),
        ],
        compiler_params=pltpu.CompilerParams(
            collective_id=0, has_side_effects=True, vmem_limit_bytes=60 * 1024 * 1024
        ),
    )(teacher_hidden, student_hidden, sampled_ids.reshape(1, 128), teacher_weight, student_weight)
    return kl.reshape(128), chosen, grad, weight_grad, hidden_grad


def solution(mesh):
    placed = (P("vocab", "row"), P("vocab", "row"), P("row", "vocab"), P("row", "vocab"), P("row"))
    return jax.shard_map(
        body,
        mesh=mesh,
        in_specs=placed,
        out_specs=(P("row"), P(None, "row"), P("row", "vocab"), P("row", "vocab"), P("vocab", "row")),
        check_vma=False,
    )
```

time: 620 us -> 127 us (0.20)
  the two profiles are of different devices: /device:TPU:1 before, /device:TPU:192 now
where the time goes in v1:
time: 127 us; the launch traced here: 126 us
  Pallas kernels  103 us (81%)
  local copies, waits for them, and re-layouts  22.6 us (18%)
    pallas_call x1, Pallas kernels, body(): pl.pallas_call(kernel, out_shape=outs, in_specs=[on_chip, on_chip, on_chi...  103 us
    unnamed x13, local copies, waits for them, and re-layouts  22.6 us

profile of v1, /device:TPU:192, one launch (start us, length us, event | category | flops | bytes accessed | tf_op | source)
XLA Modules:
  0.0 126.5 jit_solution(4045000296230965916)
XLA Ops:
  0.6 6.1 %copy.11.ws_hbm = bf16[896,2000]{1,0:T(8,128)(2,1)} copy(bf16[896,2000]{0,1:T(8,128)(2,1)} %param.8) | data formatting | bytes 7168000 | tf_op args[3]
  6.8 6.7 %copy.10.wt_hbm = bf16[1152,2000]{1,0:T(8,128)(2,1)} copy(bf16[1152,2000]{0,1:T(8,128)(2,1)} %param.7) | data formatting | bytes 9216000 | tf_op args[2]
  13.5 103.2 %shard_map.92 = (f32[1,128]{1,0:T(1,128)}, f32[2,128]{1,0:T(2,128)}, bf16[128,2000]{1,0:T(8,128)(2,1)}, bf16[896,2000]{1,0:T(8,128)(2,1)}, bf16[8,896]{1,0:T(8,128)(2,1)}) custom-call(bf16[8,1152]{1,0:T(8,128)(2,1)} %th.1, bf16[8,896]{1,0:T(8,128)(2,1)} %sh.1, s32[1,128]{1,0:T(1,128)} %bitcast.2, bf16[1152,2000]{1,0:T(8,128)(2,1)} %copy.10.wt_hbm, ...), custom_call_target="tpu_custom_call" | custom-call | tf_op jit(solution)/shard_map/pallas_call | solution.py:447
  116.7 2.1 %copy.12 = bf16[128,2000]{0,1:T(8,128)(2,1)} copy(bf16[128,2000]{1,0:T(8,128)(2,1)} %get-tuple-element.17) | data formatting | bytes 1024000
  118.8 0.0 copy-start.2
  118.8 0.0 copy-start.1
  118.8 0.0 copy-start
  118.8 6.0 %copy.13 = bf16[896,2000]{0,1:T(8,128)(2,1)} copy(bf16[896,2000]{1,0:T(8,128)(2,1)} %get-tuple-element.18) | data formatting | bytes 7168000
  124.8 0.0 copy-done.2
  124.8 0.5 copy.17
  125.3 0.0 copy-done.1
  125.3 0.6 copy.18
  125.9 0.0 copy-done
  125.9 0.6 copy.19
Async XLA Ops:
  118.8 6.0 %copy-start.2 = (f32[1,128]{1,0:T(1,128)S(1)}, f32[1,128]{1,0:T(1,128)}, u32[]{:S(2)}) copy-start(f32[1,128]{1,0:T(1,128)} %get-tuple-element.10) | copy-start | bytes 1540
  118.8 6.6 %copy-start.1 = (f32[2,128]{1,0:T(2,128)S(1)}, f32[2,128]{1,0:T(2,128)}, u32[]{:S(2)}) copy-start(f32[2,128]{1,0:T(2,128)} %get-tuple-element.26) | copy-start | bytes 3076
  118.8 7.1 %copy-start = (bf16[8,896]{1,0:T(8,128)(2,1)S(1)}, bf16[8,896]{1,0:T(8,128)(2,1)}, u32[]{:S(2)}) copy-start(bf16[8,896]{1,0:T(8,128)(2,1)} %get-tuple-element.29) | copy-start | bytes 43012

commit v2 on v1

--- a/solution.py
+++ b/solution.py
@@ -43,7 +43,7 @@
     th, sh, ids, wt_hbm, ws_hbm,
     kl_out, chosen_out, grad_out, wg_out, hg_out,
     wt, ws, ht, hs, lt, ls, part, one_s, one_r, two_s, two_r, logits, stat, ids_at, sr1, sr2, res, res_at, back,
-    grads, wg_acc, wg_stage, hp, hc, ysum, yr, zs, zr,
+    grads, wg_acc, wg_stage, grad_stage, hp, hc, ysum, yr, zs, zr,
     w_sem, zsnd, zrcv, ysnd, yrcv, csnd, crcv,
     one_ss, one_rs, two_ss, two_rs, s1_ss, s1_rs, s2_ss, s2_rs, g_ss, g_rs, f_ss, f_rs,
     hc_ss, hc_rs, hy_ss, hy_rs, hz_ss, hz_rs, out_sem,
@@ -138,7 +138,9 @@
         rows, weight = (ls, ws) if m == 0 else (lt, wt)
         lhs = rows[half, chunk]
         for lo, hi in BLOCKS:
-            part[slot, :, lo:hi] = jnp.dot(lhs, weight[:, lo:hi], preferred_element_type=F32)
+            part[slot, :, lo:hi] = lax.dot_general(
+                lhs, weight[lo:hi, :], (((1,), (1,)), ((), ())), preferred_element_type=F32
+            )
 
     def hop_one(m, half):
         u = 2 * half + m
@@ -261,7 +263,6 @@
                 jnp.exp(student) * inverse * (student - teacher + shift) * (1.0 - ratio * ratio)
             ).astype(BF16)
             grads[half, x, at, :] = value
-            grad_out[here, :] = value[:, :COLS]
 
         mine = grads.at[half, x]
         remote(mine, mine, g_ss.at[half, 0], g_rs.at[half, 0], at_x(right)).start()
@@ -285,26 +286,31 @@
     def hidden_product(half):
         rows = all_rows(half)
         for lo, hi in ((0, 256), (256, 512), (512, 768), (768, 896)):
-            block = lax.dot_general(
-                rows, ws[lo:hi, :], (((1,), (1,)), ((), ())), preferred_element_type=F32
-            )
+            block = jnp.dot(rows, ws[:, lo:hi], preferred_element_type=F32)
             hp[half, :, :, :, :, lo:hi] = block.reshape(4, 4, 2, 8, hi - lo)
         remote(
             hp.at[half, :, :, 1 - c], hc.at[half], hc_ss.at[half], hc_rs.at[half], at_v(y, z, 1 - c)
         ).start()
 
     def weight_product(half):
-        rows = all_rows(half)
-
-        @pl.loop(0, 7)
+        rows = ls[half].reshape(NX * ROWS, ls.shape[-1])
+
+        @pl.loop(0, WIDE // 256)
         def _(i):
-            at = pl.ds(pl.multiple_of(i * 128, 128), 128)
-            lhs = ls[half, :, :, at].reshape(NX * ROWS, 128)
+            at = pl.ds(pl.multiple_of(i * 256, 256), 256)
+            lhs = grads[half, :, :, at].reshape(NX * ROWS, 256)
             block = lax.dot_general(lhs, rows, (((0,), (0,)), ((), ())), preferred_element_type=F32)
             if half == 0:
                 wg_acc[at, :] = block
             else:
                 wg_stage[at, :] = (wg_acc[at, :] + block).astype(BF16)
+
+    def own_gradient():
+        @pl.loop(0, WIDE // 128)
+        def _(i):
+            at = pl.ds(pl.multiple_of(i * 128, 128), 128)
+            block = jnp.concatenate([grads[0, x, :, at], grads[1, x, :, at]], axis=0)
+            grad_stage[at, :] = jnp.transpose(block.astype(F32)).astype(BF16)
 
     def hidden_y(half):
         landed(hc.at[half], hc_rs.at[half])
@@ -394,15 +400,19 @@
     gathered(1)
     hidden_product(1)
     weight_product(1)
-    store = pltpu.make_async_copy(wg_stage, wg_out, out_sem)
+    store = pltpu.make_async_copy(wg_stage.at[pl.ds(0, COLS)], wg_out, out_sem.at[0])
     store.start()
     hidden_y(1)
+    own_gradient()
+    store_grad = pltpu.make_async_copy(grad_stage.at[pl.ds(0, COLS)], grad_out, out_sem.at[1])
+    store_grad.start()
     hidden_z(1)
     lane = lax.broadcasted_iota(jnp.int32, (1, 128), 1)
     kl_out[...] = jnp.where(lane < ROWS, back[0, 0:1, :], back[1, 0:1, :])
     chosen_out[...] = jnp.where(lane < ROWS, back[0, 1:3, :], back[1, 1:3, :])
     hidden_end(1)
     store.wait()
+    store_grad.wait()
 
     for m, ref in both:
         for step in range(1, 8):
@@ -440,17 +450,17 @@
     outs = (
         jax.ShapeDtypeStruct((1, 128), F32),
         jax.ShapeDtypeStruct((2, 128), F32),
-        jax.ShapeDtypeStruct((128, COLS), BF16),
-        jax.ShapeDtypeStruct((ks, COLS), BF16),
+        jax.ShapeDtypeStruct((COLS, 128), BF16),
+        jax.ShapeDtypeStruct((COLS, ks), BF16),
         jax.ShapeDtypeStruct((8, ks), BF16),
     )
     kl, chosen, grad, weight_grad, hidden_grad = pl.pallas_call(
         kernel,
         out_shape=outs,
         in_specs=[on_chip, on_chip, on_chip, any_space, any_space],
-        out_specs=(on_chip, on_chip, on_chip, any_space, on_chip),
+        out_specs=(on_chip, on_chip, any_space, any_space, on_chip),
         scratch_shapes=[
-            vmem((kt, COLS), BF16), vmem((ks, COLS), BF16),
+            vmem((COLS, kt), BF16), vmem((COLS, ks), BF16),
             vmem((4, 8, 2, 8, kt), BF16), vmem((4, 8, 2, 8, ks), BF16),
             vmem((2, 4, ROWS, kt), BF16), vmem((2, 4, ROWS, ks), BF16),
             vmem((3, ROWS, WIDE), F32),
@@ -461,7 +471,7 @@
             vmem((2, 8, 8, 128), F32), vmem((2, 8, 8, 128), F32),
             vmem((128, 128), F32), vmem((128, 128), F32), vmem((2, 8, 128), F32),
             vmem((2, 4, ROWS, WIDE), BF16),
-            vmem((ks, COLS), F32), vmem((ks, COLS), BF16),
+            vmem((WIDE, ks), F32), vmem((WIDE, ks), BF16), vmem((WIDE, 128), BF16),
             vmem((2, 4, 4, 2, 8, ks), F32), vmem((2, 4, 4, 8, ks), F32),
             vmem((2, 4, 32, ks), BF16), vmem((2, 4, 32, ks), BF16),
             vmem((2, 4, 8, ks), F32), vmem((8, 8, ks), F32),
@@ -469,13 +479,13 @@
             dma((4, 2)), dma((4, 2)), dma((4, 2)), dma((4, 2)),
             dma((2, 8)), dma((2, 8)), dma((2, 8)), dma((2, 8)),
             dma((2, 2)), dma((2, 2)), dma((2, 2)), dma((2, 2)),
-            dma((2,)), dma((2,)), dma((2, 4)), dma((2, 4)), dma((2, 4)), dma((8,)), dma(()),
+            dma((2,)), dma((2,)), dma((2, 4)), dma((2, 4)), dma((2, 4)), dma((8,)), dma((2,)),
         ],
         compiler_params=pltpu.CompilerParams(
             collective_id=0, has_side_effects=True, vmem_limit_bytes=60 * 1024 * 1024
         ),
-    )(teacher_hidden, student_hidden, sampled_ids.reshape(1, 128), teacher_weight, student_weight)
-    return kl.reshape(128), chosen, grad, weight_grad, hidden_grad
+    )(teacher_hidden, student_hidden, sampled_ids.reshape(1, 128), teacher_weight.T, student_weight.T)
+    return kl.reshape(128), chosen, grad.T, weight_grad.T, hidden_grad
 
 
 def solution(mesh):

time: 127 us -> 114 us (0.90)
  local copies, waits for them, and re-layouts: 22.6 us -> 8.88 us
    unnamed x13 -> x7, local copies, waits for them, and re-layouts: 22.6 us -> 8.88 us
where the time goes in v2:
time: 114 us
  Pallas kernels  104 us (91%)
  local copies, waits for them, and re-layouts  8.88 us (8%)
    pallas_call x1, Pallas kernels, body(): pl.pallas_call(kernel, out_shape=outs, in_specs=[on_chip, on_chip, on_chi...  104 us
    unnamed x7, local copies, waits for them, and re-layouts  8.88 us

profile of v2, /device:TPU:192, one launch (start us, length us, event | category | flops | bytes accessed | tf_op | source)
XLA Modules:
  0.0 113.9 jit_solution(7914555588751443731)
XLA Ops:
  0.6 104.4 %shard_map.92 = (f32[1,128]{1,0:T(1,128)}, f32[2,128]{1,0:T(2,128)}, bf16[2000,128]{1,0:T(8,128)(2,1)}, bf16[2000,896]{1,0:T(8,128)(2,1)}, bf16[8,896]{1,0:T(8,128)(2,1)}) custom-call(bf16[8,1152]{1,0:T(8,128)(2,1)} %th.1, bf16[8,896]{1,0:T(8,128)(2,1)} %sh.1, s32[1,128]{1,0:T(1,128)} %bitcast.10, bf16[2000,1152]{1,0:T(8,128)(2,1)} %bitcast.6, ...), custom_call_target="tpu_custom_call" | custom-call | tf_op jit(solution)/shard_map/pallas_call | solution.py:457
  105.0 1.1 copy.15
  106.1 1.2 %copy.16 = f32[2,128]{1,0:T(2,128)} copy(f32[2,128]{1,0:T(2,128)} %get-tuple-element.21) | data formatting | bytes 2048
  107.3 1.9 %copy.17 = bf16[128,2000]{0,1:T(8,128)(2,1)} copy(bf16[128,2000]{0,1:T(8,128)(2,1)} %bitcast.9) | data formatting | bytes 1024000
  109.2 0.0 copy-start
  109.2 4.1 %copy.18 = bf16[896,2000]{0,1:T(8,128)(2,1)} copy(bf16[896,2000]{0,1:T(8,128)(2,1)} %bitcast.8) | data formatting | bytes 7168000
  113.3 0.0 copy-done
  113.3 0.6 copy.19
Async XLA Ops:
  109.2 4.1 %copy-start = (bf16[8,896]{1,0:T(8,128)(2,1)S(1)}, bf16[8,896]{1,0:T(8,128)(2,1)}, u32[]{:S(2)}) copy-start(bf16[8,896]{1,0:T(8,128)(2,1)} %get-tuple-element.24) | copy-start | bytes 43012

commit v3 on v2

--- a/solution.py
+++ b/solution.py
@@ -264,19 +264,20 @@
             ).astype(BF16)
             grads[half, x, at, :] = value
 
-        mine = grads.at[half, x]
-        remote(mine, mine, g_ss.at[half, 0], g_rs.at[half, 0], at_x(right)).start()
-        remote(mine, mine, g_ss.at[half, 1], g_rs.at[half, 1], at_x(left)).start()
+        for turn in (0, 1):
+            for side, to in ((0, right), (1, left)):
+                mine = grads.at[half, x, pl.ds(32 * ((side + turn) % 2), 32)]
+                remote(mine, mine, g_ss.at[half, side, turn], g_rs.at[half, side, turn], at_x(to)).start()
 
     def forward(half):
-        landed(grads.at[half, left], g_rs.at[half, 0])
-        src = grads.at[half, left, pl.ds(0, 32)]
-        remote(src, src, f_ss.at[half, 0], f_rs.at[half, 0], at_x(right)).start()
-        landed(grads.at[half, right], g_rs.at[half, 1])
-        src = grads.at[half, right, pl.ds(32, 32)]
-        remote(src, src, f_ss.at[half, 1], f_rs.at[half, 1], at_x(left)).start()
+        for side, chunk, to in ((0, left, right), (1, right, left)):
+            src = grads.at[half, chunk, pl.ds(32 * side, 32)]
+            landed(src, g_rs.at[half, side, 0])
+            remote(src, src, f_ss.at[half, side], f_rs.at[half, side], at_x(to)).start()
 
     def gathered(half):
+        landed(grads.at[half, left, pl.ds(32, 32)], g_rs.at[half, 0, 1])
+        landed(grads.at[half, right, pl.ds(0, 32)], g_rs.at[half, 1, 1])
         landed(grads.at[half, across, pl.ds(0, 32)], f_rs.at[half, 0])
         landed(grads.at[half, across, pl.ds(32, 32)], f_rs.at[half, 1])
 
@@ -329,7 +330,7 @@
         for step in (1, 2, 3):
             landed(yr.at[half, step], hy_rs.at[half, step])
             total = total + yr[half, step].astype(F32)
-        zs[half] = total.reshape(4, 8, 896)
+        zs[half] = total.reshape(4, 8, 896).astype(BF16)
         for k in range(4):
             zz = 4 * half + k
 
@@ -346,70 +347,75 @@
             for step in range(1, 8):
                 who = (z + step) % 8
                 landed(zr.at[who], hz_rs.at[who])
-            total = zr[0]
+            total = zr[0].astype(F32)
             for k in range(1, 8):
-                total = total + zr[k]
+                total = total + zr[k].astype(F32)
             hg_out[...] = total.astype(BF16)
 
-    for m, ref in both:
-        for half in range(HALVES):
-            z_arrive(m, ref, half)
-            y_send(m, ref, half)
+    S, T = 0, 1
     for half in range(HALVES):
-        y_arrive(0, hs, half)
-        c_send(0, hs, half)
-    c_arrive(0, hs, 0)
-    layout(0, hs, ls, 0)
+        z_arrive(S, hs, half)
+        y_send(S, hs, half)
+    y_arrive(S, hs, 0)
+    c_send(S, hs, 0)
+    for half in range(HALVES):
+        z_arrive(T, ht, half)
+        y_send(T, ht, half)
+    c_arrive(S, hs, 0)
+    layout(S, hs, ls, 0)
     load_s.wait()
-    hop_one(0, 0)
-    c_arrive(0, hs, 1)
-    layout(0, hs, ls, 1)
-    for half in range(HALVES):
-        y_arrive(1, ht, half)
-        c_send(1, ht, half)
+    hop_one(S, 0)
+    y_arrive(S, hs, 1)
+    c_send(S, hs, 1)
+    c_arrive(S, hs, 1)
+    layout(S, hs, ls, 1)
+    hop_one(S, 1)
+    y_arrive(T, ht, 0)
+    c_send(T, ht, 0)
+    hop_two(S, 0)
     load_t.wait()
-    c_arrive(1, ht, 0)
-    layout(1, ht, lt, 0)
-    hop_one(1, 0)
-    c_arrive(1, ht, 1)
-    layout(1, ht, lt, 1)
-    hop_two(0, 0)
-    hop_one(0, 1)
-    hop_two(1, 0)
-    hop_one(1, 1)
-    finish(0, 0)
-    hop_two(0, 1)
-    finish(1, 0)
+    c_arrive(T, ht, 0)
+    layout(T, ht, lt, 0)
+    hop_one(T, 0)
+    y_arrive(T, ht, 1)
+    c_send(T, ht, 1)
+    c_arrive(T, ht, 1)
+    layout(T, ht, lt, 1)
+    hop_one(T, 1)
+    hop_two(T, 0)
+    hop_two(S, 1)
+    hop_two(T, 1)
+    finish(S, 0)
+    finish(T, 0)
     stats_one(0)
-    hop_two(1, 1)
+    finish(S, 1)
     stats_two(0)
-    finish(0, 1)
     gradient(0)
-    finish(1, 1)
+    finish(T, 1)
     stats_one(1)
     forward(0)
     stats_two(1)
+    gradient(1)
     gathered(0)
     hidden_product(0)
-    gradient(1)
+    forward(1)
     hidden_y(0)
     weight_product(0)
+    own_gradient()
+    store_grad = pltpu.make_async_copy(grad_stage.at[pl.ds(0, COLS)], grad_out, out_sem.at[1])
+    store_grad.start()
     hidden_z(0)
-    forward(1)
-    hidden_end(0)
     gathered(1)
     hidden_product(1)
+    hidden_y(1)
     weight_product(1)
     store = pltpu.make_async_copy(wg_stage.at[pl.ds(0, COLS)], wg_out, out_sem.at[0])
     store.start()
-    hidden_y(1)
-    own_gradient()
-    store_grad = pltpu.make_async_copy(grad_stage.at[pl.ds(0, COLS)], grad_out, out_sem.at[1])
-    store_grad.start()
     hidden_z(1)
     lane = lax.broadcasted_iota(jnp.int32, (1, 128), 1)
     kl_out[...] = jnp.where(lane < ROWS, back[0, 0:1, :], back[1, 0:1, :])
     chosen_out[...] = jnp.where(lane < ROWS, back[0, 1:3, :], back[1, 1:3, :])
+    hidden_end(0)
     hidden_end(1)
     store.wait()
     store_grad.wait()
@@ -430,7 +436,8 @@
             left_here(sr1.at[half, group], s1_ss.at[half, step])
             left_here(sr2.at[half, z], s2_ss.at[half, step])
         for side in (0, 1):
-            left_here(grads.at[half, x], g_ss.at[half, side])
+            for turn in (0, 1):
+                left_here(grads.at[half, x, pl.ds(0, 32)], g_ss.at[half, side, turn])
             left_here(grads.at[half, x, pl.ds(0, 32)], f_ss.at[half, side])
         left_here(hc.at[half], hc_ss.at[half])
         for step in (1, 2, 3):
@@ -440,6 +447,28 @@
             @pl.when(4 * half + k != z)
             def _():
                 left_here(zs.at[half, k], hz_ss.at[half, k])
+
+
+PIECES = tuple((lo, min(lo + 256, COLS)) for lo in range(0, COLS, 256))
+
+
+def hand_on(kl, chosen, grad, wg, hg, kl_out, chosen_out, grad_out, wg_out, hg_out, wg_here, grad_here, sems):
+    first, second = [], []
+    for source, here, target, pieces in ((wg, wg_here, wg_out, PIECES), (grad, grad_here, grad_out, ((0, COLS),))):
+        for lo, hi in pieces:
+            i = len(first)
+            first.append(pltpu.make_async_copy(source.at[lo:hi], here.at[lo:hi], sems.at[0, i]))
+            second.append(pltpu.make_async_copy(here.at[lo:hi], target.at[lo:hi], sems.at[1, i]))
+    for copy in first:
+        copy.start()
+    kl_out[...] = kl[...]
+    chosen_out[...] = chosen[...]
+    hg_out[...] = hg[...]
+    for one, two in zip(first, second):
+        one.wait()
+        two.start()
+    for copy in second:
+        copy.wait()
 
 
 def body(teacher_hidden, student_hidden, teacher_weight, student_weight, sampled_ids):
@@ -454,7 +483,7 @@
         jax.ShapeDtypeStruct((COLS, ks), BF16),
         jax.ShapeDtypeStruct((8, ks), BF16),
     )
-    kl, chosen, grad, weight_grad, hidden_grad = pl.pallas_call(
+    results = pl.pallas_call(
         kernel,
         out_shape=outs,
         in_specs=[on_chip, on_chip, on_chip, any_space, any_space],
@@ -474,17 +503,26 @@
             vmem((WIDE, ks), F32), vmem((WIDE, ks), BF16), vmem((WIDE, 128), BF16),
             vmem((2, 4, 4, 2, 8, ks), F32), vmem((2, 4, 4, 8, ks), F32),
             vmem((2, 4, 32, ks), BF16), vmem((2, 4, 32, ks), BF16),
-            vmem((2, 4, 8, ks), F32), vmem((8, 8, ks), F32),
+            vmem((2, 4, 8, ks), BF16), vmem((8, 8, ks), BF16),
             dma((2,)), dma((2, 8)), dma((2, 8)), dma((2, 2, 4)), dma((2, 2, 4)), dma((2, 2)), dma((2, 2)),
             dma((4, 2)), dma((4, 2)), dma((4, 2)), dma((4, 2)),
             dma((2, 8)), dma((2, 8)), dma((2, 8)), dma((2, 8)),
-            dma((2, 2)), dma((2, 2)), dma((2, 2)), dma((2, 2)),
+            dma((2, 2, 2)), dma((2, 2, 2)), dma((2, 2)), dma((2, 2)),
             dma((2,)), dma((2,)), dma((2, 4)), dma((2, 4)), dma((2, 4)), dma((8,)), dma((2,)),
         ],
         compiler_params=pltpu.CompilerParams(
             collective_id=0, has_side_effects=True, vmem_limit_bytes=60 * 1024 * 1024
         ),
     )(teacher_hidden, student_hidden, sampled_ids.reshape(1, 128), teacher_weight.T, student_weight.T)
+    specs = (on_chip, on_chip, any_space, any_space, on_chip)
+    kl, chosen, grad, weight_grad, hidden_grad = pl.pallas_call(
+        hand_on,
+        out_shape=outs,
+        in_specs=specs,
+        out_specs=specs,
+        scratch_shapes=[vmem((COLS, ks), BF16), vmem((COLS, 128), BF16), dma((2, len(PIECES) + 1))],
+        compiler_params=pltpu.CompilerParams(vmem_limit_bytes=60 * 1024 * 1024),
+    )(*results)
     return kl.reshape(128), chosen, grad.T, weight_grad.T, hidden_grad
 
 

time: 114 us -> 105 us (0.921)
  the two profiles are of different devices: /device:TPU:192 before, /device:TPU:1 now
where the time goes in v3:
time: 105 us; the launch traced here: 104 us
  Pallas kernels  104 us (99%)
    pallas_call x1, Pallas kernels, body(): pl.pallas_call(kernel, out_shape=outs, in_specs=[on_chip, on_chip, on_chi...  98.6 us
    pallas_call x1, Pallas kernels, body(): pl.pallas_call(hand_on, out_shape=outs, in_specs=specs, out_specs=specs,...  4.89 us

profile of v3, /device:TPU:1, one launch (start us, length us, event | category | flops | bytes accessed | tf_op | source)
XLA Modules:
  0.0 104.3 jit_solution(4174489672238224802)
XLA Ops:
  0.6 98.6 %shard_map.92 = (f32[1,128]{1,0:T(1,128)}, f32[2,128]{1,0:T(2,128)}, bf16[2000,128]{1,0:T(8,128)(2,1)}, bf16[2000,896]{1,0:T(8,128)(2,1)}, bf16[8,896]{1,0:T(8,128)(2,1)}) custom-call(bf16[8,1152]{1,0:T(8,128)(2,1)} %th.1, bf16[8,896]{1,0:T(8,128)(2,1)} %sh.1, s32[1,128]{1,0:T(1,128)} %bitcast.8, bf16[2000,1152]{1,0:T(8,128)(2,1)} %bitcast.6, ...), custom_call_target="tpu_custom_call" | custom-call | tf_op jit(solution)/shard_map/pallas_call | solution.py:486
  99.3 4.9 %shard_map.93 = (f32[1,128]{1,0:T(1,128)}, f32[2,128]{1,0:T(2,128)}, bf16[2000,128]{1,0:T(8,128)(2,1)}, bf16[2000,896]{1,0:T(8,128)(2,1)}, bf16[8,896]{1,0:T(8,128)(2,1)}) custom-call(f32[1,128]{1,0:T(1,128)} %get-tuple-element.15.kl, f32[2,128]{1,0:T(2,128)} %get-tuple-element.16.chosen, bf16[2000,128]{1,0:T(8,128)(2,1)} %get-tuple-element.17.grad, ...), custom_call_target="tpu_custom_call" | custom-call | tf_op jit(solution)/shard_map/pallas_call | solution.py:518

commit v4 on v3

v4 whole, which is shorter than its diff:
```python
import jax
import jax.numpy as jnp
from jax import lax
from jax.experimental import pallas as pl
from jax.experimental.pallas import tpu as pltpu
from jax.sharding import PartitionSpec as P

MESH = pl.DeviceIdType.MESH
F32, BF16, I16 = jnp.float32, jnp.bfloat16, jnp.int16
NX, NY, NZ, NC = 4, 4, 8, 2
OWN = 128
PARTS = ((0, 64), (64, 32), (96, 32))
COLS = 2000
WIDE = 2048
TAIL = WIDE - 128
GROUP = 16
SCALE = 32000.0
BLOCKS = ((0, 512), (512, 1024), (1024, 1536), (1536, COLS))


def softcap(values):
    return 30.0 * jnp.tanh(values * (1.0 / 30.0))


def encode(values, ref, at):
    most = jnp.max(jnp.abs(values), axis=1, keepdims=True)
    power = jnp.ceil(jnp.log2(jnp.maximum(most, 1e-30)))
    whole = jnp.round(values * (jnp.exp2(-power) * SCALE))
    lane = lax.broadcasted_iota(jnp.int32, (values.shape[0], 128), 1)
    last = jnp.where(lane >= COLS - TAIL, power, whole[:, TAIL:])
    ref[at, 0:TAIL] = whole[:, :TAIL].astype(I16)
    ref[at, TAIL:WIDE] = last.astype(I16)


def decode(ref, at):
    values = ref[at, :].astype(F32)
    lane = lax.broadcasted_iota(jnp.int32, (values.shape[0], 128), 1)
    power = jnp.max(jnp.where(lane >= COLS - TAIL, values[:, TAIL:], -1000.0), axis=1, keepdims=True)
    return values * (jnp.exp2(power) * (1.0 / SCALE))


def kernel(
    th, sh, ids, wt_hbm, ws_hbm,
    kl_out, chosen_out, grad_out, wg_out, hg_out,
    wt, ws, ht, hs, lt, ls, part, own_part, one_s, one_r, two_s, two_r, logits, stat, ids_at, sr1, sr2, res, res_at, back,
    grads, wg_acc, wg_stage, grad_stage, hb, yr, zs, zr,
    ids_here, w_sem, zsnd, zrcv, ysnd, yrcv, csnd, crcv,
    one_ss, one_rs, two_ss, two_rs, s1_ss, s1_rs, s2_ss, s2_rs, g_ss, g_rs, f_ss, f_rs,
    hy_ss, hy_rs, hz_ss, hz_rs, out_sem,
):
    x = lax.axis_index("row")
    v = lax.axis_index("vocab")
    y, z, c = v // 16, (v // 2) % 8, v % 2
    right, left, across = (x + 1) % 4, (x + 3) % 4, (x + 2) % 4

    def at_x(to):
        return (to, v)

    def at_v(ty, tz, tc):
        return (x, ty * 16 + tz * 2 + tc)

    def remote(src, dst, ss, rs, device):
        return pltpu.make_async_remote_copy(
            src_ref=src, dst_ref=dst, send_sem=ss, recv_sem=rs, device_id=device, device_id_type=MESH
        )

    def landed(ref, sem):
        remote(ref, ref, sem, sem, at_x(right)).wait_recv()

    def left_here(ref, sem):
        remote(ref, ref, sem, sem, at_x(right)).wait_send()

    barrier = pltpu.get_barrier_semaphore()
    for to in (right, left):
        pl.semaphore_signal(barrier, inc=1, device_id=at_x(to), device_id_type=MESH)
    for step in range(1, 8):
        pl.semaphore_signal(
            barrier, inc=1, device_id=at_v((y + step // 2) % 4, z, (c + step) % 2), device_id_type=MESH
        )
        pl.semaphore_signal(barrier, inc=1, device_id=at_v(y, (z + step) % 8, c), device_id_type=MESH)

    loads = [
        pltpu.make_async_copy(source, target, w_sem.at[i])
        for i, (source, target) in enumerate(
            ((sh, hs.at[y, z, c]), (th, ht.at[y, z, c]), (ids, ids_here), (ws_hbm, ws), (wt_hbm, wt))
        )
    ]
    for load in loads:
        load.start()
    part[:, :, TAIL:WIDE] = jnp.zeros((3, OWN, 128), F32)
    own_part[:, :, TAIL:WIDE] = jnp.zeros((2, OWN, 128), F32)
    stat[...] = jnp.zeros((128, 128), F32)
    res[...] = jnp.zeros((128, 128), F32)
    for load in loads[:3]:
        load.wait()
    ids_at[...] = jnp.transpose(jnp.broadcast_to(ids_here[...].astype(F32), (128, 128)))

    pl.semaphore_wait(barrier, 16)

    both = ((0, hs), (1, ht))
    for m, ref in both:
        for step in range(1, 8):
            to = (z + step) % 8
            remote(
                ref.at[y, z, c], ref.at[y, z, c], zsnd.at[m, step], zrcv.at[m, z], at_v(y, to, c)
            ).start()

    def block_rows(b):
        first, rows = PARTS[b]
        return first // 16, rows // 16

    def z_arrive(m, ref, b):
        first, count = block_rows(b)
        for zz in range(first, first + count):

            @pl.when(zz != z)
            def _():
                landed(ref.at[y, zz, c], zrcv.at[m, zz])

    def y_send(m, ref, b):
        src = ref.at[y, pl.ds(*block_rows(b)), c]
        for step in (1, 3, 2):
            remote(
                src, src, ysnd.at[m, b, step], yrcv.at[m, b, y], at_v((y + step) % 4, z, c)
            ).start()

    def y_arrive(m, ref, b):
        for step in (1, 3, 2):
            yy = (y + step) % 4
            landed(ref.at[yy, pl.ds(*block_rows(b)), c], yrcv.at[m, b, yy])

    def c_send(m, ref, b):
        src = ref.at[:, pl.ds(*block_rows(b)), c]
        remote(src, src, csnd.at[m, b], crcv.at[m, b], at_v(y, z, 1 - c)).start()

    def c_arrive(m, ref, b):
        first, count = block_rows(b)
        landed(ref.at[:, pl.ds(first, count), 1 - c], crcv.at[m, b])
        rows = (ls, lt)[m]
        for k in range(4):
            block = ref[k, first : first + count].astype(F32)
            rows[k, 16 * first : 16 * (first + count), :] = block.reshape(16 * count, rows.shape[-1]).astype(BF16)

    def product(m, b, chunks, targets):
        first, count = PARTS[b]
        rows, weight = (ls, ws) if m == 0 else (lt, wt)
        lhs = jnp.concatenate([rows[chunk, first : first + count, :] for chunk in chunks], axis=0)
        for lo, hi in BLOCKS:
            block = lax.dot_general(
                lhs, weight[lo:hi, :], (((1,), (1,)), ((), ())), preferred_element_type=F32
            )
            for i, target in enumerate(targets):
                target[first : first + count, lo:hi] = block[i * count : (i + 1) * count, :]

    def hop_one(m, b):
        first, count = PARTS[b]
        product(m, b, (across, x), (part.at[0], own_part.at[m]))

        @pl.loop(0, count // GROUP)
        def _(g):
            at = pl.ds(pl.multiple_of(first + g * GROUP, GROUP), GROUP)
            encode(part[0, at, :], one_s.at[m], at)

        some = count // 2
        for side, to in ((0, right), (1, left)):
            remote(
                one_s.at[m, pl.ds(first + side * some, some)], one_r.at[m, side, pl.ds(first // 2, some)],
                one_ss.at[m, b, side], one_rs.at[m, b, side], at_x(to),
            ).start()

    def hop_two(m, b):
        first, count = PARTS[b]
        some = count // 2
        product(m, b, (right, left), (part.at[1], part.at[2]))
        for side, to in ((0, right), (1, left)):
            landed(one_r.at[m, side, pl.ds(first // 2, some)], one_rs.at[m, b, side])

            @pl.loop(0, some // GROUP)
            def _(g):
                inner = pl.ds(pl.multiple_of(first // 2 + g * GROUP, GROUP), GROUP)
                at = pl.ds(pl.multiple_of(first + side * some + g * GROUP, GROUP), GROUP)
                plain = pl.ds(pl.multiple_of(first + (1 - side) * some + g * GROUP, GROUP), GROUP)
                encode(part[1 + side, at, :] + decode(one_r.at[m, side], inner), two_s.at[m, side], at)
                encode(part[1 + side, plain, :], two_s.at[m, side], plain)

            at = pl.ds(first, count)
            remote(
                two_s.at[m, side, at], two_r.at[m, side, at], two_ss.at[m, b, side], two_rs.at[m, b, side], at_x(to)
            ).start()

    def finish(m, b):
        first, count = PARTS[b]
        for side in (0, 1):
            landed(two_r.at[m, side, pl.ds(first, count)], two_rs.at[m, b, side])
        column = lax.broadcasted_iota(jnp.int32, (GROUP, WIDE), 1)
        lane = lax.broadcasted_iota(jnp.int32, (GROUP, 128), 1)

        @pl.loop(0, count // GROUP)
        def _(g):
            at = pl.ds(pl.multiple_of(first + g * GROUP, GROUP), GROUP)
            raw = own_part[m, at, :] + decode(two_r.at[m, 0], at) + decode(two_r.at[m, 1], at)
            capped = softcap(raw)
            logits[m, at, :] = capped
            if m == 1:
                student = logits[0, at, :]
                valid = column < COLS
                t_exp = jnp.where(valid, jnp.exp(capped), 0.0)
                s_exp = jnp.where(valid, jnp.exp(student), 0.0)
                wanted = ids_at[at, 0:1].astype(jnp.int32) - v * COLS
                hit = jnp.logical_and(column == wanted, valid)
                sums = (
                    t_exp,
                    jnp.where(hit, capped, 0.0),
                    s_exp,
                    s_exp * (student - capped),
                    jnp.where(hit, student, 0.0),
                )
                tile = jnp.zeros((GROUP, 128), F32)
                for j, term in enumerate(sums):
                    tile = jnp.where(lane == j, jnp.sum(term, axis=1, keepdims=True), tile)
                stat[at, :] = tile

    group = y * 2 + c

    def stats_one(half):
        sr1[half, group] = jnp.transpose(stat[...])[0:8, :]
        for step in range(1, 8):
            remote(
                sr1.at[half, group], sr1.at[half, group], s1_ss.at[half, step], s1_rs.at[half, group],
                at_v((y + step // 2) % 4, z, (c + step) % 2),
            ).start()

    def stats_two(half):
        for step in range(1, 8):
            who = ((y + step // 2) % 4) * 2 + (c + step) % 2
            landed(sr1.at[half, who], s1_rs.at[half, who])
        total = sr1[half, 0]
        for k in range(1, 8):
            total = total + sr1[half, k]
        sr2[half, z] = total
        for step in range(1, 8):
            remote(
                sr2.at[half, z], sr2.at[half, z], s2_ss.at[half, step], s2_rs.at[half, z],
                at_v(y, (z + step) % 8, c),
            ).start()

    def gradient(half):
        for step in range(1, 8):
            who = (z + step) % 8
            landed(sr2.at[half, who], s2_rs.at[half, who])
        total = sr2[half, 0]
        for k in range(1, 8):
            total = total + sr2[half, k]
        t_total, t_pick, s_total, cross, s_pick = (total[j : j + 1, :] for j in range(5))
        s_log, t_log = jnp.log(s_total), jnp.log(t_total)
        divergence = cross / s_total - s_log + t_log
        res[0:1, :] = 1.0 / s_total
        res[1:2, :] = t_log - s_log - divergence
        back[half, 0:1, :] = divergence
        back[half, 1:2, :] = s_pick - s_log
        back[half, 2:3, :] = t_pick - t_log
        res_at[...] = jnp.transpose(res[...])

        first, count = PARTS[half]

        @pl.loop(0, count // GROUP)
        def _(g):
            at = pl.ds(pl.multiple_of(first + g * GROUP, GROUP), GROUP)
            student, teacher = logits[0, at, :], logits[1, at, :]
            inverse, shift = res_at[at, 0:1], res_at[at, 1:2]
            ratio = student * (1.0 / 30.0)
            grads[x, at, :] = (
                jnp.exp(student) * inverse * (student - teacher + shift) * (1.0 - ratio * ratio)
            ).astype(BF16)

        some = count // 2
        for turn in (0, 1):
            for side, to in ((0, right), (1, left)):
                mine = grads.at[x, pl.ds(first + some * ((side + turn) % 2), some)]
                remote(mine, mine, g_ss.at[half, side, turn], g_rs.at[half, side, turn], at_x(to)).start()

    def forward(b):
        first, count = PARTS[b]
        some = count // 2
        for side, chunk, to in ((0, left, right), (1, right, left)):
            src = grads.at[chunk, pl.ds(first + some * side, some)]
            landed(src, g_rs.at[b, side, 0])
            remote(src, src, f_ss.at[b, side], f_rs.at[b, side], at_x(to)).start()

    def gathered(b):
        first, count = PARTS[b]
        some = count // 2
        landed(grads.at[left, pl.ds(first + some, some)], g_rs.at[b, 0, 1])
        landed(grads.at[right, pl.ds(first, some)], g_rs.at[b, 1, 1])
        landed(grads.at[across, pl.ds(first, some)], f_rs.at[b, 0])
        landed(grads.at[across, pl.ds(first + some, some)], f_rs.at[b, 1])

    def hidden_product(b):
        first, count = PARTS[b]
        rows = grads[:, first : first + count, 0:COLS].reshape(NX * count, COLS)
        at = slice(first // 2, (first + count) // 2)
        for lo, hi in ((0, 256), (256, 512), (512, 768), (768, 896)):
            block = jnp.dot(rows, ws[:, lo:hi], preferred_element_type=F32)
            block = block.reshape(4, count // 16, 2, 8, hi - lo)
            for k in range(4):
                for core in range(2):
                    hb[k, core, at, lo:hi] = block[k, :, core].reshape(count // 2, hi - lo).astype(BF16)
        at = pl.ds(first // 2, count // 2)
        for step in range(1, 8):
            ty, tc = (y + step // 2) % 4, (c + step) % 2
            remote(
                hb.at[ty, tc, at], yr.at[group, at], hy_ss.at[b, step], hy_rs.at[b, group], at_v(ty, z, tc)
            ).start()

    def weight_product(half):
        rows = ls[:, half * 64 : half * 64 + 64, :].reshape(NX * 64, ls.shape[-1])

        @pl.loop(0, WIDE // 256)
        def _(i):
            at = pl.ds(pl.multiple_of(i * 256, 256), 256)
            lhs = grads[:, half * 64 : half * 64 + 64, at].reshape(NX * 64, 256)
            block = lax.dot_general(lhs, rows, (((0,), (0,)), ((), ())), preferred_element_type=F32)
            if half == 0:
                wg_acc[at, :] = block
            else:
                wg_stage[at, :] = (wg_acc[at, :] + block).astype(BF16)

    def own_gradient():
        @pl.loop(0, WIDE // 128)
        def _(i):
            at = pl.ds(pl.multiple_of(i * 128, 128), 128)
            grad_stage[at, :] = jnp.transpose(grads[x, :, at].astype(F32)).astype(BF16)

    def hidden_z(b):
        first, count = block_rows(b)
        at = pl.ds(8 * first, 8 * count)
        total = hb[y, c, 8 * first : 8 * (first + count), :].astype(F32)
        for step in range(1, 8):
            who = ((y + step // 2) % 4) * 2 + (c + step) % 2
            landed(yr.at[who, at], hy_rs.at[b, who])
            total = total + yr[who, 8 * first : 8 * (first + count), :].astype(F32)
        zs[first : first + count] = total.reshape(count, 8, 896).astype(BF16)
        for zz in range(first, first + count):

            @pl.when(zz != z)
            def _():
                remote(zs.at[zz], zr.at[z], hz_ss.at[zz], hz_rs.at[z], at_v(y, zz, c)).start()

    def hidden_end():
        zr[z] = zs[z]
        for step in range(1, 8):
            who = (z + step) % 8
            landed(zr.at[who], hz_rs.at[who])
        total = zr[0].astype(F32)
        for k in range(1, 8):
            total = total + zr[k].astype(F32)
        hg_out[...] = total.astype(BF16)

    S, T = 0, 1
    for b in range(3):
        z_arrive(S, hs, b)
        y_send(S, hs, b)
    y_arrive(S, hs, 0)
    c_send(S, hs, 0)
    for b in range(3):
        z_arrive(T, ht, b)
        y_send(T, ht, b)
    c_arrive(S, hs, 0)
    loads[3].wait()
    hop_one(S, 0)
    for b in (1, 2):
        y_arrive(S, hs, b)
        c_send(S, hs, b)
    for b in (1, 2):
        c_arrive(S, hs, b)
        hop_one(S, b)
    y_arrive(T, ht, 0)
    c_send(T, ht, 0)
    hop_two(S, 0)
    loads[4].wait()
    c_arrive(T, ht, 0)
    hop_one(T, 0)
    for b in (1, 2):
        y_arrive(T, ht, b)
        c_send(T, ht, b)
    hop_two(S, 1)
    hop_two(T, 0)
    for b in (1, 2):
        c_arrive(T, ht, b)
        hop_one(T, b)
    finish(S, 0)
    hop_two(S, 2)
    finish(T, 0)
    stats_one(0)
    hop_two(T, 1)
    hop_two(T, 2)
    finish(S, 1)
    stats_two(0)
    finish(T, 1)
    stats_one(1)
    finish(S, 2)
    gradient(0)
    stats_two(1)
    finish(T, 2)
    stats_one(2)
    gradient(1)
    forward(0)
    stats_two(2)
    forward(1)
    gradient(2)
    gathered(0)
    hidden_product(0)
    forward(2)
    gathered(1)
    hidden_product(1)
    own_gradient()
    store_grad = pltpu.make_async_copy(grad_stage.at[pl.ds(0, COLS)], grad_out, out_sem.at[1])
    store_grad.start()
    hidden_z(0)
    weight_product(0)
    gathered(2)
    hidden_product(2)
    hidden_z(1)
    weight_product(1)
    store = pltpu.make_async_copy(wg_stage.at[pl.ds(0, COLS)], wg_out, out_sem.at[0])
    store.start()
    hidden_z(2)
    lane = lax.broadcasted_iota(jnp.int32, (1, 128), 1)
    final = back[0]
    for b in (1, 2):
        final = jnp.where(lane < PARTS[b][0], final, back[b])
    kl_out[...] = final[0:1, :]
    chosen_out[...] = final[1:3, :]
    hidden_end()
    store.wait()
    store_grad.wait()

    for m, ref in both:
        for step in range(1, 8):
            left_here(ref.at[y, z, c], zsnd.at[m, step])
        for b in range(3):
            for step in (1, 2, 3):
                left_here(ref.at[y, pl.ds(*block_rows(b)), c], ysnd.at[m, b, step])
            left_here(ref.at[:, pl.ds(*block_rows(b)), c], csnd.at[m, b])
    for m in (0, 1):
        for b, (first, count) in enumerate(PARTS):
            for side in (0, 1):
                left_here(one_s.at[m, pl.ds(first, count // 2)], one_ss.at[m, b, side])
                left_here(two_s.at[m, side, pl.ds(first, count)], two_ss.at[m, b, side])
    for b, (first, count) in enumerate(PARTS):
        for step in range(1, 8):
            left_here(sr1.at[b, group], s1_ss.at[b, step])
            left_here(sr2.at[b, z], s2_ss.at[b, step])
            left_here(hb.at[y, c, pl.ds(first // 2, count // 2)], hy_ss.at[b, step])
        for side in (0, 1):
            left_here(grads.at[x, pl.ds(first, count // 2)], f_ss.at[b, side])
            for turn in (0, 1):
                left_here(grads.at[x, pl.ds(first, count // 2)], g_ss.at[b, side, turn])
    for zz in range(8):

        @pl.when(zz != z)
        def _():
            left_here(zs.at[zz], hz_ss.at[zz])


PIECES = tuple((lo, min(lo + 256, COLS)) for lo in range(0, COLS, 256))


def hand_on(*refs):
    sources, targets, here, sems = refs[:5], refs[5:10], refs[10:15], refs[15]
    first, second = [], []
    for k, (source, target, stage) in enumerate(zip(sources, targets, here)):
        for lo, hi in PIECES if k == 3 else ((0, source.shape[0]),):
            i = len(first)
            first.append(pltpu.make_async_copy(source.at[lo:hi], stage.at[lo:hi], sems.at[0, i]))
            second.append(pltpu.make_async_copy(stage.at[lo:hi], target.at[lo:hi], sems.at[1, i]))
    for copy in first:
        copy.start()
    for one, two in zip(first, second):
        one.wait()
        two.start()
    for copy in second:
        copy.wait()


def body(teacher_hidden, student_hidden, teacher_weight, student_weight, sampled_ids):
    dma, vmem = pltpu.SemaphoreType.DMA, pltpu.VMEM
    on_chip = pl.BlockSpec(memory_space=pltpu.VMEM)
    any_space = pl.BlockSpec(memory_space=pl.ANY)
    kt, ks = teacher_weight.shape[0], student_weight.shape[0]
    outs = (
        jax.ShapeDtypeStruct((1, 128), F32),
        jax.ShapeDtypeStruct((2, 128), F32),
        jax.ShapeDtypeStruct((COLS, 128), BF16),
        jax.ShapeDtypeStruct((COLS, ks), BF16),
        jax.ShapeDtypeStruct((8, ks), BF16),
    )
    results = pl.pallas_call(
        kernel,
        out_shape=outs,
        in_specs=[any_space] * 5,
        out_specs=(on_chip, on_chip, any_space, any_space, on_chip),
        scratch_shapes=[
            vmem((COLS, kt), BF16), vmem((COLS, ks), BF16),
            vmem((4, 8, 2, 8, kt), BF16), vmem((4, 8, 2, 8, ks), BF16),
            vmem((4, OWN, kt), BF16), vmem((4, OWN, ks), BF16),
            vmem((3, OWN, WIDE), F32), vmem((2, OWN, WIDE), F32),
            vmem((2, OWN, WIDE), I16), vmem((2, 2, OWN // 2, WIDE), I16),
            vmem((2, 2, OWN, WIDE), I16), vmem((2, 2, OWN, WIDE), I16),
            vmem((2, OWN, WIDE), F32),
            vmem((128, 128), F32), vmem((128, 128), F32),
            vmem((3, 8, 8, 128), F32), vmem((3, 8, 8, 128), F32),
            vmem((128, 128), F32), vmem((128, 128), F32), vmem((3, 8, 128), F32),
            vmem((4, OWN, WIDE), BF16),
            vmem((WIDE, ks), F32), vmem((WIDE, ks), BF16), vmem((WIDE, 128), BF16),
            vmem((4, 2, OWN // 2, ks), BF16), vmem((8, OWN // 2, ks), BF16),
            vmem((8, 8, ks), BF16), vmem((8, 8, ks), BF16), vmem((1, 128), jnp.int32),
            dma((5,)), dma((2, 8)), dma((2, 8)), dma((2, 3, 4)), dma((2, 3, 4)), dma((2, 3)), dma((2, 3)),
            dma((2, 3, 2)), dma((2, 3, 2)), dma((2, 3, 2)), dma((2, 3, 2)),
            dma((3, 8)), dma((3, 8)), dma((3, 8)), dma((3, 8)),
            dma((3, 2, 2)), dma((3, 2, 2)), dma((3, 2)), dma((3, 2)),
            dma((3, 8)), dma((3, 8)), dma((8,)), dma((8,)), dma((2,)),
        ],
        compiler_params=pltpu.CompilerParams(
            collective_id=0, has_side_effects=True, vmem_limit_bytes=60 * 1024 * 1024
        ),
    )(teacher_hidden, student_hidden, sampled_ids.reshape(1, 128), teacher_weight.T, student_weight.T)
    kl, chosen, grad, weight_grad, hidden_grad = pl.pallas_call(
        hand_on,
        out_shape=outs,
        in_specs=[any_space] * 5,
        out_specs=[any_space] * 5,
        scratch_shapes=[vmem(out.shape, out.dtype) for out in outs] + [dma((2, len(PIECES) + 4))],
        compiler_params=pltpu.CompilerParams(vmem_limit_bytes=60 * 1024 * 1024),
    )(*results)
    return kl.reshape(128), chosen, grad.T, weight_grad.T, hidden_grad


def solution(mesh):
    placed = (P("vocab", "row"), P("vocab", "row"), P("row", "vocab"), P("row", "vocab"), P("row"))
    return jax.shard_map(
        body,
        mesh=mesh,
        in_specs=placed,
        out_specs=(P("row"), P(None, "row"), P("row", "vocab"), P("row", "vocab"), P("vocab", "row")),
        check_vma=False,
    )
```

time: 105 us -> 103 us (0.981)
  Pallas kernels: 104 us -> 102 us
    pallas_call x2, Pallas kernels: 104 us -> 102 us  [the longest x1 98.7 us: body(): pl.pallas_call(kernel, out_shape=outs, in_specs=[any_space] * 5, out_spec...]
where the time goes in v4:
time: 103 us
  Pallas kernels  102 us (99%)
    pallas_call x1, Pallas kernels, body(): pl.pallas_call(kernel, out_shape=outs, in_specs=[any_space] * 5, out_spec...  98.7 us
    pallas_call x1, Pallas kernels, body(): pl.pallas_call(hand_on, out_shape=outs, in_specs=[any_space] * 5, out_spe...  3.52 us

profile of v4, /device:TPU:1, one launch (start us, length us, event | category | flops | bytes accessed | tf_op | source)
XLA Modules:
  0.0 102.8 jit_solution(8337666256909792395)
XLA Ops:
  0.6 98.7 %shard_map.92 = (f32[1,128]{1,0:T(1,128)}, f32[2,128]{1,0:T(2,128)}, bf16[2000,128]{1,0:T(8,128)(2,1)}, bf16[2000,896]{1,0:T(8,128)(2,1)}, bf16[8,896]{1,0:T(8,128)(2,1)}) custom-call(bf16[8,1152]{1,0:T(8,128)(2,1)} %th.1, bf16[8,896]{1,0:T(8,128)(2,1)} %sh.1, s32[1,128]{1,0:T(1,128)} %bitcast.8, bf16[2000,1152]{1,0:T(8,128)(2,1)} %bitcast.6, ...), custom_call_target="tpu_custom_call" | custom-call | tf_op jit(solution)/shard_map/pallas_call | solution.py:498
  99.3 3.5 %shard_map.93 = (f32[1,128]{1,0:T(1,128)}, f32[2,128]{1,0:T(2,128)}, bf16[2000,128]{1,0:T(8,128)(2,1)}, bf16[2000,896]{1,0:T(8,128)(2,1)}, bf16[8,896]{1,0:T(8,128)(2,1)}) custom-call(f32[1,128]{1,0:T(1,128)} %get-tuple-element.15.refs_0_, f32[2,128]{1,0:T(2,128)} %get-tuple-element.16.refs_1_, bf16[2000,128]{1,0:T(8,128)(2,1)} %get-tuple-element.17.refs_2_, ...), custom_call_target="tpu_custom_call" | custom-call | tf_op jit(solution)/shard_map/pallas_call | solution.py:528

commit v5 on v4

--- a/solution.py
+++ b/solution.py
@@ -14,6 +14,7 @@
 WIDE = 2048
 TAIL = WIDE - 128
 GROUP = 16
+FAR_FIRST = (4, 3, 5, 2, 6, 1, 7)
 SCALE = 32000.0
 BLOCKS = ((0, 512), (512, 1024), (1024, 1536), (1536, COLS))
 
@@ -73,7 +74,7 @@
     barrier = pltpu.get_barrier_semaphore()
     for to in (right, left):
         pl.semaphore_signal(barrier, inc=1, device_id=at_x(to), device_id_type=MESH)
-    for step in range(1, 8):
+    for step in FAR_FIRST:
         pl.semaphore_signal(
             barrier, inc=1, device_id=at_v((y + step // 2) % 4, z, (c + step) % 2), device_id_type=MESH
         )
@@ -98,12 +99,14 @@
     pl.semaphore_wait(barrier, 16)
 
     both = ((0, hs), (1, ht))
-    for m, ref in both:
-        for step in range(1, 8):
+    def z_send(m, ref):
+        for step in FAR_FIRST:
             to = (z + step) % 8
             remote(
                 ref.at[y, z, c], ref.at[y, z, c], zsnd.at[m, step], zrcv.at[m, z], at_v(y, to, c)
             ).start()
+
+    z_send(0, hs)
 
     def block_rows(b):
         first, rows = PARTS[b]
@@ -224,7 +227,7 @@
 
     def stats_one(half):
         sr1[half, group] = jnp.transpose(stat[...])[0:8, :]
-        for step in range(1, 8):
+        for step in FAR_FIRST:
             remote(
                 sr1.at[half, group], sr1.at[half, group], s1_ss.at[half, step], s1_rs.at[half, group],
                 at_v((y + step // 2) % 4, z, (c + step) % 2),
@@ -238,7 +241,7 @@
         for k in range(1, 8):
             total = total + sr1[half, k]
         sr2[half, z] = total
-        for step in range(1, 8):
+        for step in FAR_FIRST:
             remote(
                 sr2.at[half, z], sr2.at[half, z], s2_ss.at[half, step], s2_rs.at[half, z],
                 at_v(y, (z + step) % 8, c),
@@ -357,7 +360,10 @@
         hg_out[...] = total.astype(BF16)
 
     S, T = 0, 1
-    for b in range(3):
+    z_arrive(S, hs, 0)
+    y_send(S, hs, 0)
+    z_send(T, ht)
+    for b in (1, 2):
         z_arrive(S, hs, b)
         y_send(S, hs, b)
     y_arrive(S, hs, 0)
@@ -403,8 +409,8 @@
     stats_two(1)
     finish(T, 2)
     stats_one(2)
+    forward(0)
     gradient(1)
-    forward(0)
     stats_two(2)
     forward(1)
     gradient(2)

time: 103 us -> 99.6 us (0.967)
  Pallas kernels: 102 us -> 98.8 us
    pallas_call x1, Pallas kernels: 98.7 us -> 95.3 us  [body(): pl.pallas_call(kernel, out_shape=outs, in_specs=[any_space] * 5, out_spec...]
where the time goes in v5:
time: 99.6 us; the launch traced here: 99.4 us
  Pallas kernels  98.8 us (99%)
    pallas_call x1, Pallas kernels, body(): pl.pallas_call(kernel, out_shape=outs, in_specs=[any_space] * 5, out_spec...  95.3 us
    pallas_call x1, Pallas kernels, body(): pl.pallas_call(hand_on, out_shape=outs, in_specs=[any_space] * 5, out_spe...  3.52 us

profile of v5, /device:TPU:1, one launch (start us, length us, event | category | flops | bytes accessed | tf_op | source)
XLA Modules:
  0.0 99.4 jit_solution(3085320745022254508)
XLA Ops:
  0.6 95.3 %shard_map.92 = (f32[1,128]{1,0:T(1,128)}, f32[2,128]{1,0:T(2,128)}, bf16[2000,128]{1,0:T(8,128)(2,1)}, bf16[2000,896]{1,0:T(8,128)(2,1)}, bf16[8,896]{1,0:T(8,128)(2,1)}) custom-call(bf16[8,1152]{1,0:T(8,128)(2,1)} %th.1, bf16[8,896]{1,0:T(8,128)(2,1)} %sh.1, s32[1,128]{1,0:T(1,128)} %bitcast.8, bf16[2000,1152]{1,0:T(8,128)(2,1)} %bitcast.6, ...), custom_call_target="tpu_custom_call" | custom-call | tf_op jit(solution)/shard_map/pallas_call | solution.py:504
  95.9 3.5 %shard_map.93 = (f32[1,128]{1,0:T(1,128)}, f32[2,128]{1,0:T(2,128)}, bf16[2000,128]{1,0:T(8,128)(2,1)}, bf16[2000,896]{1,0:T(8,128)(2,1)}, bf16[8,896]{1,0:T(8,128)(2,1)}) custom-call(f32[1,128]{1,0:T(1,128)} %get-tuple-element.15.refs_0_, f32[2,128]{1,0:T(2,128)} %get-tuple-element.16.refs_1_, bf16[2000,128]{1,0:T(8,128)(2,1)} %get-tuple-element.17.refs_2_, ...), custom_call_target="tpu_custom_call" | custom-call | tf_op jit(solution)/shard_map/pallas_call | solution.py:534

commit v6 on v5

--- a/solution.py
+++ b/solution.py
@@ -15,6 +15,7 @@
 TAIL = WIDE - 128
 GROUP = 16
 FAR_FIRST = (4, 3, 5, 2, 6, 1, 7)
+BESIDE = (5, 4, 2, 3, 6, 7, 1)
 SCALE = 32000.0
 BLOCKS = ((0, 512), (512, 1024), (1024, 1536), (1536, COLS))
 
@@ -122,13 +123,13 @@
 
     def y_send(m, ref, b):
         src = ref.at[y, pl.ds(*block_rows(b)), c]
-        for step in (1, 3, 2):
+        for step in (2, 1, 3):
             remote(
                 src, src, ysnd.at[m, b, step], yrcv.at[m, b, y], at_v((y + step) % 4, z, c)
             ).start()
 
     def y_arrive(m, ref, b):
-        for step in (1, 3, 2):
+        for step in (2, 1, 3):
             yy = (y + step) % 4
             landed(ref.at[yy, pl.ds(*block_rows(b)), c], yrcv.at[m, b, yy])
 
@@ -227,7 +228,7 @@
 
     def stats_one(half):
         sr1[half, group] = jnp.transpose(stat[...])[0:8, :]
-        for step in FAR_FIRST:
+        for step in BESIDE:
             remote(
                 sr1.at[half, group], sr1.at[half, group], s1_ss.at[half, step], s1_rs.at[half, group],
                 at_v((y + step // 2) % 4, z, (c + step) % 2),
@@ -309,7 +310,7 @@
                 for core in range(2):
                     hb[k, core, at, lo:hi] = block[k, :, core].reshape(count // 2, hi - lo).astype(BF16)
         at = pl.ds(first // 2, count // 2)
-        for step in range(1, 8):
+        for step in BESIDE:
             ty, tc = (y + step // 2) % 4, (c + step) % 2
             remote(
                 hb.at[ty, tc, at], yr.at[group, at], hy_ss.at[b, step], hy_rs.at[b, group], at_v(ty, z, tc)

time: 99.6 us -> 98.7 us (level)
  no operation moved by 1% of the time
where the time goes in v6:
time: 98.7 us; the launch traced here: 98.6 us
  Pallas kernels  97.9 us (99%)
    pallas_call x1, Pallas kernels, body(): pl.pallas_call(kernel, out_shape=outs, in_specs=[any_space] * 5, out_spec...  94.4 us
    pallas_call x1, Pallas kernels, body(): pl.pallas_call(hand_on, out_shape=outs, in_specs=[any_space] * 5, out_spe...  3.52 us

profile of v6, /device:TPU:1, one launch (start us, length us, event | category | flops | bytes accessed | tf_op | source)
XLA Modules:
  0.0 98.6 jit_solution(15688264928245077734)
XLA Ops:
  0.6 94.4 %shard_map.92 = (f32[1,128]{1,0:T(1,128)}, f32[2,128]{1,0:T(2,128)}, bf16[2000,128]{1,0:T(8,128)(2,1)}, bf16[2000,896]{1,0:T(8,128)(2,1)}, bf16[8,896]{1,0:T(8,128)(2,1)}) custom-call(bf16[8,1152]{1,0:T(8,128)(2,1)} %th.1, bf16[8,896]{1,0:T(8,128)(2,1)} %sh.1, s32[1,128]{1,0:T(1,128)} %bitcast.8, bf16[2000,1152]{1,0:T(8,128)(2,1)} %bitcast.6, ...), custom_call_target="tpu_custom_call" | custom-call | tf_op jit(solution)/shard_map/pallas_call | solution.py:505
  95.1 3.5 %shard_map.93 = (f32[1,128]{1,0:T(1,128)}, f32[2,128]{1,0:T(2,128)}, bf16[2000,128]{1,0:T(8,128)(2,1)}, bf16[2000,896]{1,0:T(8,128)(2,1)}, bf16[8,896]{1,0:T(8,128)(2,1)}) custom-call(f32[1,128]{1,0:T(1,128)} %get-tuple-element.15.refs_0_, f32[2,128]{1,0:T(2,128)} %get-tuple-element.16.refs_1_, bf16[2000,128]{1,0:T(8,128)(2,1)} %get-tuple-element.17.refs_2_, ...), custom_call_target="tpu_custom_call" | custom-call | tf_op jit(solution)/shard_map/pallas_call | solution.py:535
